TPU v7x, 32 devices: a whole 2x2x4 slice. The times are simulated.
32 devices in a mesh: groups: 2 (over y), tensor: 4 (over z), batch: 2 (over x), rep: 2 (over core).
Axes of the slice: x: 2, y: 2, z: 4, core: 2. Of those that a mesh axis runs over, the one named last changes fastest.
Arguments:
- ri_tensor: bfloat16 [64, 64, 4096], P(('groups', 'tensor')), parts along dimension 0, may hold values from -0.29882812 to 0.29882812
- pair_ids: int32 [512], P(('groups', 'tensor')), parts along dimension 0, may hold values from 0 to 255, as said below
- atom_size: int32 [16], replicated, may hold values from 32 to 64
- green_occ: bfloat16 [1024, 1024], replicated, may hold values from -0.1875 to 0.1875
- green_virt: bfloat16 [1024, 1024], P(None, ('batch', 'rep')), may hold values from -0.375 to 0.375
Outputs:
- response: float32 [64, 32], P(('groups', 'tensor'), ('batch', 'rep')), parts along dimension 0
There are 2 independent parts, one for each index of `groups`. A program takes and returns all parts, laid end to end along the dimension named above; an argument that names none is the same for every part. Nothing has to cross between parts.
Inputs may be any that keep to these rules, and one draw needn't show every extreme that they name: `pair_ids`: entry e names the atom pair (e // 16, e % 16); the 64 entries of one tensor index are distinct.
All inputs are finite; a program needn't handle non-finite values.
Results may differ from a plain program's by a relative error of at most 0.012.
Values may be sent and summed in bfloat16 or wider, within the bound.
A program may use at most 192 MiB of HBM per device.

v0:
```python
import jax
import jax.numpy as jnp
from jax import lax
from jax.sharding import PartitionSpec as P

NAT = 16
BS = 64


def per_device(ri_tensor, pair_ids, atom_size, green_occ, green_virt):
    local_rows = ri_tensor.shape[0]
    slots = ri_tensor.shape[1]
    total_ao = green_occ.shape[0]
    columns = green_virt.shape[1]
    first_col = (lax.axis_index("batch") * lax.axis_size("rep") + lax.axis_index("rep")) * columns
    usable = (jnp.arange(BS)[None, :] < atom_size[:, None]).astype(jnp.bfloat16)
    row_atoms = pair_ids // NAT
    col_atoms = pair_ids % NAT
    blocks = ri_tensor.reshape(local_rows, slots, BS, BS)
    blocks = blocks * usable[row_atoms][None, :, :, None] * usable[col_atoms][None, :, None, :]
    selector_f = row_atoms[None, :] == jnp.arange(NAT)[:, None]
    selector = selector_f.astype(jnp.bfloat16)
    block_cols = col_atoms[:, None] * BS + jnp.arange(BS)[None, :]
    wanted = first_col + jnp.arange(columns)
    picker = (block_cols[:, :, None] == wanted[None, None, :]).astype(jnp.bfloat16)
    picked = jnp.einsum(
        "psij,sjk->psik", blocks, picker, preferred_element_type=jnp.float32
    ).astype(jnp.bfloat16)
    tensor_piece = jnp.einsum("as,psik->paik", selector, picked, preferred_element_type=jnp.float32)
    tensor_piece = tensor_piece.astype(jnp.bfloat16).reshape(local_rows, total_ao, columns)
    gv_blocks = green_virt.reshape(NAT, BS, columns)[col_atoms]
    per_slot = jnp.einsum("psij,sjk->psik", blocks, gv_blocks, preferred_element_type=jnp.float32)
    upper = per_slot.astype(jnp.bfloat16)
    rest = per_slot - upper.astype(jnp.float32)
    middle = rest.astype(jnp.bfloat16)
    lower = (rest - middle.astype(jnp.float32)).astype(jnp.bfloat16)
    virt_side = jnp.einsum("as,psik->paik", selector, upper, preferred_element_type=jnp.float32)
    virt_side = virt_side + jnp.einsum(
        "as,psik->paik", selector, middle, preferred_element_type=jnp.float32
    )
    virt_side = virt_side + jnp.einsum(
        "as,psik->paik", selector, lower, preferred_element_type=jnp.float32
    )
    virt_side = virt_side.astype(jnp.bfloat16).reshape(local_rows, total_ao, columns)
    occ_side = jnp.einsum(
        "lm,pms->pls", green_occ, virt_side, preferred_element_type=jnp.float32
    ).astype(jnp.bfloat16)
    moved_occ, moved_tensor = (
        lax.all_to_all(occ_side, "tensor", split_axis=1, concat_axis=0, tiled=True),
        lax.all_to_all(tensor_piece, "tensor", split_axis=1, concat_axis=0, tiled=True),
    )
    partial_value = jnp.einsum(
        "pls,qls->pq", moved_occ, moved_tensor, preferred_element_type=jnp.float32
    )
    own_rows = lax.psum_scatter(partial_value, "tensor", scatter_dimension=0, tiled=True)
    return lax.psum_scatter(own_rows, ("batch", "rep"), scatter_dimension=1, tiled=True)


def solution(mesh):
    in_specs = (
        P(("groups", "tensor"), None, None),
        P(("groups", "tensor")),
        P(),
        P(),
        P(None, ("batch", "rep")),
    )
    out_specs = P(("groups", "tensor"), ("batch", "rep"))
    return jax.shard_map(
        per_device, mesh=mesh, in_specs=in_specs, out_specs=out_specs, check_vma=False
    )
```

profile of v0, /device:TPU:0, one launch (start us, length us, event | category | flops | bytes accessed | tf_op | source)
XLA Modules:
  0.0 272.7 jit_solution(8869487890038374551)
XLA Ops:
  0.0 0.0 copy-start
  0.0 0.0 copy-start.2
  0.0 0.0 copy-start.3
  0.0 12.7 %reshape.43 = bf16[8,64,64,64]{3,2,1,0:T(8,128)(2,1)} reshape(bf16[8,64,4096]{2,1,0:T(8,128)(2,1)} %param.5) | data formatting | bytes 8388608 | tf_op jit(solution)/shard_map/reshape | solution.py:19
  12.7 0.0 copy-done.2
  12.7 0.1 fusion.38
  12.8 0.0 copy-done.3
  12.8 0.6 gather_fusion.2
  13.5 0.6 gather_fusion.1
  14.1 0.1 iota_add_fusion
  14.2 10.8 %convert_bitcast_fusion = bf16[8,64,64,256]{3,2,0,1:T(8,128)(2,1)} fusion(bf16[8,64,64,64]{3,2,1,0:T(8,128)(2,1)} %reshape.43, bf16[64,64]{1,0:T(8,128)(2,1)S(1)} %gather_fusion.2, bf16[64,64]{1,0:T(8,128)(2,1)S(1)} %gather_fusion.1, s32[256]{0:T(256)S(1)} %iota_add_fusion.1, s32[64,64]{1,0:T(8,128)S(1)} %iota_add_fusion), kind=kOutput, calls=%fused_computation.15 | convolution fusion | flops 1095761920 | bytes 21005312 | tf_op jit(solution)/shard_map/psij,sjk->psik/dot_general | solution.py:26
  25.0 15.1 %convert_bitcast_fusion.1 = bf16[8,16,64,256]{3,1,2,0:T(8,128)(2,1)S(1)} fusion(bf16[8,64,64,256]{3,2,0,1:T(8,128)(2,1)} %convert_bitcast_fusion, s32[64]{0:T(128)S(1)} %get-tuple-element.8), kind=kOutput, calls=%fused_computation.26 | convolution fusion | flops 270533632 | bytes 20971776 | tf_op jit(solution)/shard_map/as,psik->paik/dot_general | solution.py:29
  40.0 1.7 copy.29
  41.8 0.0 copy-start.1
  41.8 4.6 %copy.30 = bf16[8,1024,256]{2,0,1:T(8,128)(2,1)} copy(bf16[8,1024,256]{2,1,0:T(8,128)(2,1)S(1)} %bitcast.72) | data formatting | bytes 8388608 | tf_op jit(solution)/shard_map/reshape | solution.py:30
  46.3 6.3 %all-to-all-start.1 = ((bf16[8,1024,256]{2,0,1:T(8,128)(2,1)}), bf16[8,1024,256]{2,0,1:T(8,128)(2,1)}, u32[]{:S(2)}, u32[]{:S(2)}) async-start(bf16[8,1024,256]{2,0,1:T(8,128)(2,1)} %copy.30), calls=%async_computation.1 | async-start | bytes 8388608 | tf_op jit(solution)/shard_map/all_to_all | solution.py:50
  52.7 0.0 copy-done.1
  52.7 2.0 gather_fusion
  54.7 20.8 %fusion = (bf16[8,64,64,256]{3,2,0,1:T(8,128)(2,1)}, bf16[8,64,64,256]{3,2,0,1:T(8,128)(2,1)}, bf16[64,256,8,64]{1,3,2,0:T(8,128)(2,1)}) fusion(bf16[8,64,64,64]{3,2,1,0:T(8,128)(2,1)} %reshape.43, bf16[64,64]{1,0:T(8,128)(2,1)S(1)} %gather_fusion.2, bf16[64,64]{1,0:T(8,128)(2,1)S(1)} %gather_fusion.1, bf16[64,64,256]{2,1,0:T(8,128)(2,1)} %gather_fusion), kind=kOutput, calls=%fused_computation.6 | convolution fusion | flops 1153433600 | bytes 56639488 | tf_op jit(solution)/shard_map/psij,sjk->psik/dot_general | solution.py:32
  75.5 18.1 %fusion.3 = f32[8,64,256,16]{2,3,1,0:T(8,128)} fusion(bf16[8,64,64,256]{3,2,0,1:T(8,128)(2,1)} %get-tuple-element.10, s32[64]{0:T(128)S(1)} %get-tuple-element.8), kind=kOutput, calls=%fused_computation.9 | convolution fusion | flops 268436480 | bytes 25166080 | tf_op jit(solution)/shard_map/as,psik->paik/dot_general | solution.py:41
  93.6 18.5 %fusion.5 = f32[8,64,256,16]{2,3,1,0:T(8,128)} fusion(bf16[8,64,64,256]{3,2,0,1:T(8,128)(2,1)} %get-tuple-element.9, s32[64]{0:T(128)S(1)} %get-tuple-element.8), kind=kOutput, calls=%fused_computation.11 | convolution fusion | flops 268436480 | bytes 25166080 | tf_op jit(solution)/shard_map/as,psik->paik/dot_general | solution.py:38
  112.1 19.3 %fusion.13 = bf16[8,16,64,256]{3,1,2,0:T(8,128)(2,1)S(1)} fusion(f32[8,64,256,16]{2,3,1,0:T(8,128)} %fusion.3, f32[8,64,256,16]{2,3,1,0:T(8,128)} %fusion.5, bf16[8,64,64,256]{3,2,0,1:T(8,128)(2,1)} %bitcast.71, s32[64]{0:T(128)S(1)} %get-tuple-element.8), kind=kOutput, calls=%fused_computation.20 | convolution fusion | flops 274727936 | bytes 37748992 | tf_op jit(solution)/shard_map/as,psik->paik/dot_general | solution.py:37
  131.4 1.6 copy.24
  133.0 0.0 copy-done
  133.1 6.4 %convert_bitcast_fusion.2 = bf16[8,1024,256]{1,2,0:T(8,128)(2,1)} fusion(bf16[8,1024,256]{2,1,0:T(8,128)(2,1)S(1)} %bitcast.74, bf16[1024,1024]{1,0:T(8,128)(2,1)S(1)} %copy-done), kind=kOutput, calls=%fused_computation.27 | convolution fusion | flops 4297064448 | bytes 10485760 | tf_op jit(solution)/shard_map/lm,pms->pls/dot_general | solution.py:45
  139.5 0.0 copy-start.5
  139.5 0.0 copy-start.4
  139.5 7.0 %copy.26 = bf16[8,1024,256]{2,0,1:T(8,128)(2,1)} copy(bf16[8,1024,256]{1,2,0:T(8,128)(2,1)} %convert_bitcast_fusion.2) | data formatting | bytes 8388608 | tf_op jit(solution)/shard_map/convert_element_type | solution.py:47
  146.5 0.0 all-to-all-done.1
  146.5 5.1 %all-to-all-start = ((bf16[8,1024,256]{2,0,1:T(8,128)(2,1)}), bf16[8,1024,256]{2,0,1:T(8,128)(2,1)}, u32[]{:S(2)}, u32[]{:S(2)}) async-start(bf16[8,1024,256]{2,0,1:T(8,128)(2,1)} %copy.26), calls=%async_computation | async-start | bytes 8388608 | tf_op jit(solution)/shard_map/all_to_all | solution.py:49
  151.6 0.0 copy-done.5
  151.6 0.6 dynamic-slice
  152.1 0.0 copy-done.4
  152.1 0.6 dynamic-slice.2
  154.0 90.7 %all-to-all-done = bf16[8,1024,256]{2,0,1:T(8,128)(2,1)} async-done(((bf16[8,1024,256]{2,0,1:T(8,128)(2,1)}), bf16[8,1024,256]{2,0,1:T(8,128)(2,1)}, u32[]{:S(2)}, u32[]{:S(2)}) %all-to-all-start) | async-done | bytes 4194336 | tf_op jit(solution)/shard_map/all_to_all | solution.py:49
  244.8 4.7 %fusion.33 = f32[32,32]{1,0:T(8,128)S(1)} fusion(bf16[4,8,256,256]{3,1,2,0:T(8,128)(2,1)} %bitcast.21, bf16[8,4,256,256]{3,0,2,1:T(8,128)(2,1)} %bitcast.11), kind=kOutput, calls=%fused_computation.38 | convolution fusion | flops 134217728 | bytes 8392704 | tf_op jit(solution)/shard_map/pls,qls->pq/dot_general | solution.py:52
  249.4 16.8 %all-reduce = f32[32,32]{1,0:T(8,128)S(1)} all-reduce(f32[32,32]{1,0:T(8,128)S(1)} %fusion.33), channel_id=2, replica_groups=mesh['groups'=2,'tensor'=4,'batch'=2,'rep'=2] {'tensor'}, use_global_device_ids=true, to_apply=%region_0.1.clone | all-reduce | flops 1024 | bytes 8192
  266.2 5.6 %all-reduce.1 = f32[8,32]{1,0:T(8,128)S(1)} all-reduce(f32[8,32]{1,0:T(8,128)S(1)} %constant_dynamic-slice_fusion.1), channel_id=3, replica_groups=mesh['groups'=2,'tensor'=4,'batch'=2,'rep'=2] {'batch','rep'}, use_global_device_ids=true, to_apply=%region_1.2.clone | all-reduce | flops 256 | bytes 2048
  271.9 0.7 constant_dynamic-slice_fusion
  (5 shorter events, 0.0 us)
Async XLA Ops:
  0.0 133.0 %copy-start = (bf16[1024,1024]{1,0:T(8,128)(2,1)S(1)}, bf16[1024,1024]{1,0:T(8,128)(2,1)}, u32[]{:S(2)}) copy-start(bf16[1024,1024]{1,0:T(8,128)(2,1)} %param.8) | copy-start | bytes 6291460
  0.0 12.7 %copy-start.2 = (s32[16]{0:T(128)S(1)}, s32[16]{0:T(128)}, u32[]{:S(2)}) copy-start(s32[16]{0:T(128)} %param.7) | copy-start | bytes 196
  0.0 12.8 %copy-start.3 = (s32[64]{0:T(128)S(1)}, s32[64]{0:T(128)}, u32[]{:S(2)}) copy-start(s32[64]{0:T(128)} %param.6) | copy-start | bytes 772
  41.8 10.9 %copy-start.1 = (bf16[1024,256]{1,0:T(8,128)(2,1)S(1)}, bf16[1024,256]{1,0:T(8,128)(2,1)}, u32[]{:S(2)}) copy-start(bf16[1024,256]{1,0:T(8,128)(2,1)} %param.9) | copy-start | bytes 1572868
  46.3 100.1 %all-to-all-start.1 = ((bf16[8,1024,256]{2,0,1:T(8,128)(2,1)}), bf16[8,1024,256]{2,0,1:T(8,128)(2,1)}, u32[]{:S(2)}, u32[]{:S(2)}) async-start(bf16[8,1024,256]{2,0,1:T(8,128)(2,1)} %copy.30), calls=%async_computation.1 | async-start | bytes 8388608 | tf_op jit(solution)/shard_map/all_to_all | solution.py:50
  139.5 12.1 %copy-start.5 = (u32[32]{0:T(128)S(1)}, u32[32]{0:T(128)}, u32[]{:S(2)}) copy-start(u32[32]{0:T(128)} %constant.44) | copy-start | bytes 388
  139.5 12.6 %copy-start.4 = (u32[32]{0:T(128)S(1)}, u32[32]{0:T(128)}, u32[]{:S(2)}) copy-start(u32[32]{0:T(128)} %constant.48) | copy-start | bytes 388
  146.5 98.3 %all-to-all-start = ((bf16[8,1024,256]{2,0,1:T(8,128)(2,1)}), bf16[8,1024,256]{2,0,1:T(8,128)(2,1)}, u32[]{:S(2)}, u32[]{:S(2)}) async-start(bf16[8,1024,256]{2,0,1:T(8,128)(2,1)} %copy.26), calls=%async_computation | async-start | bytes 8388608 | tf_op jit(solution)/shard_map/all_to_all | solution.py:49
where the time goes:
time: 277 us; the launch traced here: 273 us
  matrix products  114 us (41%)
  waiting for transfers between devices  90.7 us (33%)
  local copies, waits for them, and re-layouts  32.8 us (12%)
  blocking collectives  22.5 us (8%)
  starting transfers between devices  11.4 us (4%)
    all_to_all x1, waiting for transfers between devices, per_device(): lax.all_to_all(occ_side, 'tensor', split_axis=1, concat_axis=0, tiled=True)  90.7 us
    unnamed x2, blocking collectives  22.5 us
    dot_general x1, matrix products, per_device(): jnp.einsum('psij,sjk->psik', blocks, gv_blocks, preferred_element_type=jn...  20.8 us
    dot_general x1, matrix products, per_device(): jnp.einsum('as,psik->paik', selector, upper, preferred_element_type=jnp.f...  19.3 us
    dot_general x1, matrix products, per_device(): jnp.einsum('as,psik->paik', selector, middle, preferred_element_type=jnp....  18.5 us
    dot_general x1, matrix products, per_device(): jnp.einsum('as,psik->paik', selector, lower, preferred_element_type=jnp.f...  18.1 us
    dot_general x1, matrix products, per_device(): jnp.einsum('as,psik->paik', selector, picked, preferred_element_type=jnp....  15.1 us
    reshape x1, local copies, waits for them, and re-layouts, per_device(): blocks = ri_tensor.reshape(local_rows, slots, BS, BS)  12.7 us
  transfers between devices with their start and end apart: 2, of which 1 were waited for; matrix products, arithmetic and copies ran while one was open for 35% of the time, Pallas kernels for 0%

commit v1 on v0

--- a/solution.py
+++ b/solution.py
@@ -1,13 +1,381 @@
+import functools
+
 import jax
 import jax.numpy as jnp
 from jax import lax
+from jax.experimental import pallas as pl
+from jax.experimental.pallas import tpu as pltpu
 from jax.sharding import PartitionSpec as P
 
 NAT = 16
 BS = 64
+MESH = pl.DeviceIdType.MESH
+NT = (((1,), (1,)), ((), ()))
+
+
+def gather_kernel(nz, ri, ids_k, ids_n, size, go, gv, out,
+                  slabs, perm, tmp, gop, gvm, sel, dense, virt, flat, idbuf, part, parts,
+                  zsend, zrecv, xsend, xrecv, csend, crecv, isend, irecv, psend, precv, lsem):
+    z = lax.axis_index("tensor")
+    b = lax.axis_index("batch")
+    r = lax.axis_index("rep")
+    j = b * 2 + r
+    pieces = 4
+    waves = (nz - 1) * pieces
+    left = {"tensor": z - 1}
+    right = {"tensor": z + 1}
+    across = {"batch": 1 - b}
+    mate = {"rep": 1 - r}
+    diag = {"batch": 1 - b, "rep": 1 - r}
+
+    barrier = pltpu.get_barrier_semaphore()
+    for step in range(1, nz):
+        pl.semaphore_signal(barrier, inc=1, device_id={"tensor": lax.rem(z + step, nz)}, device_id_type=MESH)
+    for dev in (across, mate, diag):
+        pl.semaphore_signal(barrier, inc=1, device_id=dev, device_id_type=MESH)
+
+    def local(q):
+        return pltpu.make_async_copy(
+            ri.at[:, pl.ds(16 * q, 16), :],
+            slabs.at[z, q], lsem.at[q])
+
+    def remote(src, dst, s, d, dev):
+        return pltpu.make_async_remote_copy(src_ref=src, dst_ref=dst, send_sem=s, recv_sem=d,
+                                            device_id=dev, device_id_type=MESH)
+
+    def spot(o, p, q):
+        return slabs.at[o, q, pl.ds(2 * p, 2)]
+
+    for q in range(4):
+        local(q).start()
+    pl.semaphore_wait(barrier, nz - 1 + 3)
+
+    def own(p, d):
+        src = ri.at[pl.ds(2 * p, 2), pl.ds(pl.multiple_of(16 * j, 16), 16), :]
+        return remote(src, spot(z, p, j), zsend.at[d, p], zrecv.at[d, p], right if d == 0 else left)
+
+    def ids_copy(step):
+        dev = {"tensor": lax.rem(z + step, nz)}
+        return remote(ids_n, idbuf.at[z], isend.at[step], irecv.at[step], dev)
+
+    for step in range(1, nz):
+        ids_copy(step).start()
+    for p in range(pieces):
+        @pl.when(z < nz - 1)
+        def _():
+            own(p, 0).start()
+
+        @pl.when(z > 0)
+        def _():
+            own(p, 1).start()
+
+    def origin(d, t):
+        return z - 1 - t if d == 0 else z + 1 + t
+
+    def here(d, t):
+        return t <= z - 1 if d == 0 else t <= nz - 2 - z
+
+    def passes(d, t):
+        ok = here(d, t)
+        return jnp.logical_and(ok, z < nz - 1) if d == 0 else jnp.logical_and(ok, z > 0)
+
+    def z_copy(d, w, o, p):
+        return remote(spot(o, p, j), spot(o, p, j), zsend.at[d, w + pieces], zrecv.at[d, w + pieces],
+                      right if d == 0 else left)
+
+    def z_in(d, w, o, p):
+        return remote(spot(o, p, j), spot(o, p, j), zsend.at[d, w], zrecv.at[d, w], right if d == 0 else left)
+
+    def x_copy(d, w, o, p, q):
+        return remote(spot(o, p, q), spot(o, p, q), xsend.at[d, w], xrecv.at[d, w], across)
+
+    def c_copy(d, w, k, o, p, q):
+        return remote(spot(o, p, q), spot(o, p, q), csend.at[d, w, k], crecv.at[d, w, k], mate)
+
+    jx = (1 - b) * 2 + r
+    jm = b * 2 + 1 - r
+    jd = (1 - b) * 2 + 1 - r
+
+    def arrive(w):
+        t, p = w // pieces, w % pieces
+        for d in (0, 1):
+            @pl.when(here(d, t))
+            def _():
+                o = origin(d, t)
+                z_in(d, w, o, p).wait_recv()
+
+                @pl.when(passes(d, t))
+                def _():
+                    z_copy(d, w, o, p).start()
+                x_copy(d, w, o, p, j).start()
+                c_copy(d, w, 0, o, p, j).start()
+
+    def spread(w):
+        t, p = w // pieces, w % pieces
+        for d in (0, 1):
+            @pl.when(here(d, t))
+            def _():
+                o = origin(d, t)
+                x_copy(d, w, o, p, jx).wait_recv()
+                c_copy(d, w, 1, o, p, jx).start()
+
+    def collect(w):
+        t, p = w // pieces, w % pieces
+        for d in (0, 1):
+            @pl.when(here(d, t))
+            def _():
+                o = origin(d, t)
+                c_copy(d, w, 0, o, p, jm).wait_recv()
+                c_copy(d, w, 1, o, p, jd).wait_recv()
+
+    lane = lax.broadcasted_iota(jnp.int32, (1, 1024), 1)
+    limit = jnp.zeros((1, 1024), jnp.int32)
+    for a in range(16):
+        limit = jnp.where(lane // 64 == a, size[a], limit)
+
+    def build(k, _):
+        row = lax.broadcasted_iota(jnp.int32, (128, 1024), 0) + k * 128
+        col = lax.broadcasted_iota(jnp.int32, (128, 1024), 1)
+        place = (col % 64) * 16 + col // 64
+        keep = jnp.logical_and(place == row, col % 64 < limit)
+        perm[pl.ds(pl.multiple_of(k * 128, 128), 128), :] = jnp.where(keep, 1.0, 0.0).astype(jnp.bfloat16)
+        return 0
+
+    lax.fori_loop(0, 8, build, 0)
+
+    def rows_in(k, _):
+        at = pl.ds(pl.multiple_of(k * 256, 256), 256)
+        tmp[at, :] = jnp.dot(perm[at, :], go[...], preferred_element_type=jnp.float32).astype(jnp.bfloat16)
+        return 0
+
+    lax.fori_loop(0, 4, rows_in, 0)
+
+    def cols_in(k, _):
+        at = pl.ds(pl.multiple_of(k * 256, 256), 256)
+        gop[at, :] = lax.dot_general(tmp[at, :], perm[...], NT,
+                                     preferred_element_type=jnp.float32).astype(jnp.bfloat16)
+        return 0
+
+    lax.fori_loop(0, 4, cols_in, 0)
+
+    lane256 = lax.broadcasted_iota(jnp.int32, (64, 256), 1)
+    sub256 = lax.broadcasted_iota(jnp.int32, (64, 256), 0)
+    limit_c = jnp.zeros((64, 256), jnp.int32)
+    for c in range(4):
+        limit_c = jnp.where(lane256 // 64 == c, size[j * 4 + c], limit_c)
+    for c in range(16):
+        keep = jnp.logical_and(sub256 < size[c], lane256 % 64 < limit_c)
+        block = gv[c * 64:(c + 1) * 64, :].astype(jnp.float32)
+        gvm[c * 64:(c + 1) * 64, :] = jnp.where(keep, block, 0.0).astype(jnp.bfloat16)
+
+    row = lax.broadcasted_iota(jnp.int32, (256, 64), 0)
+    want = (row % 16) * 16 + ((row % 128) // 16) * 2 + row // 128
+    sel[...] = jnp.where(ids_k[...] == want, 1.0, 0.0).astype(jnp.bfloat16)
+    idbuf[z] = ids_n[...]
+    part[...] = jnp.zeros_like(part)
+    for q in range(4):
+        local(q).wait()
+
+    low = lax.broadcasted_iota(jnp.int32, (128, 128), 1) < 64
+    low16 = lax.broadcasted_iota(jnp.int32, (32, 128), 1) < 64
+
+    def one_function(f):
+        def unpack(k, _):
+            at = pl.ds(pl.multiple_of(k * 256, 256), 256)
+            mine = jnp.concatenate([slabs[z, q, f, :, at] for q in range(4)], axis=0)
+            got = jnp.dot(sel[...], mine, preferred_element_type=jnp.float32)
+            for h in range(2):
+                even, odd = got[:128, h * 128:(h + 1) * 128], got[128:, h * 128:(h + 1) * 128]
+                first = jnp.where(low, even, pltpu.roll(odd, 64, 1)).astype(jnp.bfloat16)
+                second = jnp.where(low, pltpu.roll(even, 64, 1), odd).astype(jnp.bfloat16)
+                base = k * 64 + h * 32
+                for c in range(8):
+                    dense[pl.ds(pl.multiple_of(base, 16), 16), c * 128:(c + 1) * 128] = first[c * 16:(c + 1) * 16]
+                    dense[pl.ds(pl.multiple_of(base + 16, 16), 16), c * 128:(c + 1) * 128] = second[c * 16:(c + 1) * 16]
+            return 0
+
+        lax.fori_loop(0, 16, unpack, 0)
+
+        def virt_step(k, _):
+            at = pl.ds(pl.multiple_of(k * 256, 256), 256)
+            virt[at, :] = jnp.dot(dense[at, :], gvm[...], preferred_element_type=jnp.float32).astype(jnp.bfloat16)
+            return 0
+
+        lax.fori_loop(0, 4, virt_step, 0)
+
+        def occ_step(k, _):
+            at = pl.ds(pl.multiple_of(k * 256, 256), 256)
+            occ = jnp.dot(gop[at, :], virt[...], preferred_element_type=jnp.float32)
+            for h in range(8):
+                even, odd = occ[h * 32:h * 32 + 16], occ[h * 32 + 16:h * 32 + 32]
+                even = jnp.concatenate([even[:, :128], even[:, 128:]], axis=0)
+                odd = jnp.concatenate([odd[:, :128], odd[:, 128:]], axis=0)
+                first = jnp.where(low16, even, pltpu.roll(odd, 64, 1)).astype(jnp.bfloat16)
+                second = jnp.where(low16, pltpu.roll(even, 64, 1), odd).astype(jnp.bfloat16)
+                lanes = pl.ds(pl.multiple_of(k * 1024 + h * 128, 128), 128)
+                flat[pl.ds(pl.multiple_of(f * 64, 32), 32), lanes] = first
+                flat[pl.ds(pl.multiple_of(f * 64 + 32, 32), 32), lanes] = second
+            return 0
+
+        lax.fori_loop(0, 4, occ_step, 0)
+
+    row64 = lax.broadcasted_iota(jnp.int32, (64, 128), 0)
+    want64 = (row64 % 16) * 16 + j * 4 + ((row64 % 32) // 16) * 2 + row64 // 32
+    out_lane = lax.broadcasted_iota(jnp.int32, (8, 128), 1)
+
+    def contract(o, p):
+        other = jnp.concatenate([slabs[o, q, pl.ds(2 * p, 2)].reshape(32, 4096) for q in range(4)], axis=0)
+        pick = idbuf[o] == want64
+        halves = jnp.zeros((8, 128), jnp.float32)
+        for m in range(2):
+            gram = lax.dot_general(flat[m * 256:(m + 1) * 256, :], other, NT, preferred_element_type=jnp.float32)
+            for f in range(4):
+                kept = jnp.sum(jnp.where(pick, gram[f * 64:(f + 1) * 64], 0.0), axis=0, keepdims=True)
+                halves = jnp.where(lax.broadcasted_iota(jnp.int32, (8, 128), 0) == m * 4 + f, kept, halves)
+        add = jnp.zeros((8, 128), jnp.float32)
+        for q in range(2):
+            total = jnp.sum(jnp.where((out_lane // 16) % 2 == q, halves, 0.0), axis=1, keepdims=True)
+            add = add + jnp.where(out_lane == o * 8 + p * 2 + q, total, 0.0)
+        part[...] += add
+
+    def contract_wave(w):
+        t, p = w // pieces, w % pieces
+        for d in (0, 1):
+            @pl.when(here(d, t))
+            def _():
+                contract(origin(d, t), p)
+
+    def first_phase(w, _):
+        one_function(2 * w)
+        arrive(w)
+
+        @pl.when(w > 0)
+        def _():
+            spread(w - 1)
+        one_function(2 * w + 1)
+        return 0
+
+    lax.fori_loop(0, 4, first_phase, 0)
+    for step in range(1, nz):
+        ids_copy(step).wait_send()
+        remote(ids_n, idbuf.at[z], isend.at[step], irecv.at[step], right).wait_recv()
+
+    def own_slab(p, _):
+        contract(z, p)
+        return 0
+
+    arrive(4)
+    spread(3)
+    lax.fori_loop(0, 2, own_slab, 0)
+    arrive(5)
+    spread(4)
+    lax.fori_loop(2, 4, own_slab, 0)
+
+    def catch_up(w, _):
+        collect(w)
+        contract_wave(w)
+        return 0
+
+    lax.fori_loop(0, 3, catch_up, 0)
+
+    def second_phase(w, _):
+        @pl.when(w < waves)
+        def _():
+            arrive(w)
+
+        @pl.when(w < waves + 1)
+        def _():
+            spread(w - 1)
+        collect(w - 3)
+        contract_wave(w - 3)
+        return 0
+
+    lax.fori_loop(6, waves + 3, second_phase, 0)
+
+    def p_copy(k, dev):
+        return remote(part, parts.at[k], psend.at[k], precv.at[k], dev)
+
+    for k, dev in enumerate((across, mate, diag)):
+        p_copy(k, dev).start()
+
+    def finish(w, _):
+        t, p = w // pieces, w % pieces
+        for d in (0, 1):
+            @pl.when(here(d, t))
+            def _():
+                o = origin(d, t)
+
+                @pl.when(passes(d, t))
+                def _():
+                    z_copy(d, w, o, p).wait_send()
+                x_copy(d, w, o, p, j).wait_send()
+                c_copy(d, w, 0, o, p, j).wait_send()
+                c_copy(d, w, 1, o, p, jx).wait_send()
+        return 0
+
+    lax.fori_loop(0, waves, finish, 0)
+    for p in range(pieces):
+        @pl.when(z < nz - 1)
+        def _():
+            own(p, 0).wait_send()
+
+        @pl.when(z > 0)
+        def _():
+            own(p, 1).wait_send()
+    for k, dev in enumerate((across, mate, diag)):
+        p_copy(k, dev).wait()
+    total = part[...] + parts[0] + parts[1] + parts[2]
+    wide = out.shape[1]
+    result = jnp.zeros(out.shape, jnp.float32)
+    for q in range(4):
+        result = jnp.where(j == q, total[:, q * wide:(q + 1) * wide], result)
+    out[...] = result
+
+
+def fused(nz, ri_tensor, pair_ids, atom_size, green_occ, green_virt):
+    ids_n = jnp.broadcast_to(pair_ids.reshape(4, 1, 16), (4, 2, 16)).reshape(1, 128)
+    waves = (nz - 1) * 4
+    vmem = pl.BlockSpec(memory_space=pltpu.VMEM)
+    bf16 = jnp.bfloat16
+    dma = pltpu.SemaphoreType.DMA
+    return pl.pallas_call(
+        functools.partial(gather_kernel, nz),
+        out_shape=jax.ShapeDtypeStruct((8, nz * 2), jnp.float32),
+        in_specs=[pl.BlockSpec(memory_space=pl.ANY), vmem, vmem,
+                  pl.BlockSpec(memory_space=pltpu.SMEM), vmem, vmem],
+        out_specs=vmem,
+        scratch_shapes=[
+            pltpu.VMEM((nz, 4, 8, 16, 4096), bf16),
+            pltpu.VMEM((1024, 1024), bf16),
+            pltpu.VMEM((1024, 1024), bf16),
+            pltpu.VMEM((1024, 1024), bf16),
+            pltpu.VMEM((1024, 256), bf16),
+            pltpu.VMEM((256, 64), bf16),
+            pltpu.VMEM((1024, 1024), bf16),
+            pltpu.VMEM((1024, 256), bf16),
+            pltpu.VMEM((512, 4096), bf16),
+            pltpu.VMEM((nz, 1, 128), jnp.int32),
+            pltpu.VMEM((8, 128), jnp.float32),
+            pltpu.VMEM((3, 8, 128), jnp.float32),
+            dma((2, waves + 4)), dma((2, waves + 4)),
+            dma((2, waves)), dma((2, waves)),
+            dma((2, waves, 2)), dma((2, waves, 2)),
+            dma((nz,)), dma((nz,)), dma((3,)), dma((3,)), dma((4,)),
+        ],
+        compiler_params=pltpu.CompilerParams(
+            collective_id=0, has_side_effects=True, vmem_limit_bytes=56 * 1024 * 1024),
+    )(ri_tensor, pair_ids.reshape(1, 64), ids_n, atom_size, green_occ, green_virt)
 
 
 def per_device(ri_tensor, pair_ids, atom_size, green_occ, green_virt):
+    nz = lax.axis_size("tensor")
+    split = (lax.axis_size("batch"), lax.axis_size("rep"))
+    if nz == 4 and split == (2, 2) and ri_tensor.shape == (8, 64, 4096) and green_occ.shape == (1024, 1024):
+        return fused(nz, ri_tensor, pair_ids, atom_size, green_occ, green_virt)
+    return whole_blocks(ri_tensor, pair_ids, atom_size, green_occ, green_virt)
+
+
+def whole_blocks(ri_tensor, pair_ids, atom_size, green_occ, green_virt):
     local_rows = ri_tensor.shape[0]
     slots = ri_tensor.shape[1]
     total_ao = green_occ.shape[0]

time: 277 us -> 129 us (0.47); the launches traced: 273 us -> 129 us
  Pallas kernels: 0 us -> 126 us
  matrix products: 114 us -> 0 us
  waiting for transfers between devices: 90.7 us -> 0 us
  local copies, waits for them, and re-layouts: 32.8 us -> 2.62 us
  blocking collectives: 22.5 us -> 0 us
  starting transfers between devices: 11.4 us -> 0 us
    pallas_call x0 -> x1, Pallas kernels: none -> 126 us  [fused(): pl.pallas_call(functools.partial(gather_kernel, nz), out_shape=jax.ShapeD...]
    dot_general x8 -> x0, matrix products: 114 us -> none  [the longest x1 20.8 us: per_device(): jnp.einsum('psij,sjk->psik', blocks, gv_blocks, preferred_element_type=jn...]
    all_to_all x2 -> x0, waiting for transfers between devices: 90.7 us -> none  [the longest x1 90.7 us: per_device(): lax.all_to_all(occ_side, 'tensor', split_axis=1, concat_axis=0, tiled=True)]
    unnamed x2 -> x0, blocking collectives: 22.5 us -> none
    reshape x2 -> x1, local copies, waits for them, and re-layouts: 17.3 us -> 0.6 us  [fused(): jnp.broadcast_to(pair_ids.reshape(4, 1, 16), (4, 2, 16)).reshape(1, 128)]
    all_to_all x2 -> x0, starting transfers between devices: 11.4 us -> none  [the longest x1 6.33 us: per_device(): lax.all_to_all(tensor_piece, 'tensor', split_axis=1, concat_axis=0, tiled...]
    convert_element_type x3 -> x0, local copies, waits for them, and re-layouts: 10.3 us -> none  [the longest x1 6.97 us: per_device(): occ_side = jnp.einsum('lm,pms->pls', green_occ, virt_side, preferred_elem...]
    gather x3 -> x0, local copies, waits for them, and re-layouts: 3.27 us -> none  [the longest x1 2 us: per_device(): gv_blocks = green_virt.reshape(NAT, BS, columns)[col_atoms]]
  transfers between devices with their start and end apart: 2 -> 0, of which waited for: 1 -> 0; matrix products, arithmetic and copies ran while one was open for 35% -> 0% of each run, Pallas kernels for 0% -> 0%
where the time goes in v1:
time: 129 us
  Pallas kernels  126 us (98%)
  local copies, waits for them, and re-layouts  2.62 us (2%)
    pallas_call x1, Pallas kernels, fused(): pl.pallas_call(functools.partial(gather_kernel, nz), out_shape=jax.ShapeD...  126 us

profile of v1, /device:TPU:0, one launch (start us, length us, event | category | flops | bytes accessed | tf_op | source)
XLA Modules:
  0.0 128.7 jit_solution(16245872593749725471)
XLA Ops:
  0.0 0.7 broadcast_in_dim.7
  0.7 0.6 reshape.9.ids_n
  1.3 126.1 %shard_map.55 = f32[8,8]{1,0:T(8,128)} custom-call(bf16[8,64,4096]{2,1,0:T(8,128)(2,1)} %ri.1, s32[1,64]{1,0:T(1,128)} %bitcast.1, s32[1,128]{1,0:T(1,128)} %reshape.9.ids_n, s32[16]{0:T(128)} %size.1, bf16[1024,1024]{1,0:T(8,128)(2,1)} %go.1, bf16[1024,256]{1,0:T(8,128)(2,1)} %gv.1), custom_call_target="tpu_custom_call" | custom-call | tf_op jit(solution)/shard_map/pallas_call | solution.py:341
  127.5 1.3 copy.7
  (1 shorter events, 0.0 us)

commit v2 on v1

--- a/solution.py
+++ b/solution.py
@@ -148,7 +148,7 @@
         tmp[at, :] = jnp.dot(perm[at, :], go[...], preferred_element_type=jnp.float32).astype(jnp.bfloat16)
         return 0
 
-    lax.fori_loop(0, 4, rows_in, 0)
+    lax.fori_loop(0, 4, rows_in, 0, unroll=True)
 
     def cols_in(k, _):
         at = pl.ds(pl.multiple_of(k * 256, 256), 256)
@@ -156,7 +156,7 @@
                                      preferred_element_type=jnp.float32).astype(jnp.bfloat16)
         return 0
 
-    lax.fori_loop(0, 4, cols_in, 0)
+    lax.fori_loop(0, 4, cols_in, 0, unroll=True)
 
     lane256 = lax.broadcasted_iota(jnp.int32, (64, 256), 1)
     sub256 = lax.broadcasted_iota(jnp.int32, (64, 256), 0)
@@ -194,14 +194,14 @@
                     dense[pl.ds(pl.multiple_of(base + 16, 16), 16), c * 128:(c + 1) * 128] = second[c * 16:(c + 1) * 16]
             return 0
 
-        lax.fori_loop(0, 16, unpack, 0)
+        lax.fori_loop(0, 16, unpack, 0, unroll=True)
 
         def virt_step(k, _):
             at = pl.ds(pl.multiple_of(k * 256, 256), 256)
             virt[at, :] = jnp.dot(dense[at, :], gvm[...], preferred_element_type=jnp.float32).astype(jnp.bfloat16)
             return 0
 
-        lax.fori_loop(0, 4, virt_step, 0)
+        lax.fori_loop(0, 4, virt_step, 0, unroll=True)
 
         def occ_step(k, _):
             at = pl.ds(pl.multiple_of(k * 256, 256), 256)
@@ -217,7 +217,7 @@
                 flat[pl.ds(pl.multiple_of(f * 64 + 32, 32), 32), lanes] = second
             return 0
 
-        lax.fori_loop(0, 4, occ_step, 0)
+        lax.fori_loop(0, 4, occ_step, 0, unroll=True)
 
     row64 = lax.broadcasted_iota(jnp.int32, (64, 128), 0)
     want64 = (row64 % 16) * 16 + j * 4 + ((row64 % 32) // 16) * 2 + row64 // 32

time: 129 us -> 105 us (0.81)
  Pallas kernels: 126 us -> 103 us
    pallas_call x1, Pallas kernels: 126 us -> 103 us  [fused(): pl.pallas_call(functools.partial(gather_kernel, nz), out_shape=jax.ShapeD...]
where the time goes in v2:
time: 105 us
  Pallas kernels  103 us (98%)
  local copies, waits for them, and re-layouts  2.62 us (2%)
    pallas_call x1, Pallas kernels, fused(): pl.pallas_call(functools.partial(gather_kernel, nz), out_shape=jax.ShapeD...  103 us

profile of v2, /device:TPU:0, one launch (start us, length us, event | category | flops | bytes accessed | tf_op | source)
XLA Modules:
  0.0 105.2 jit_solution(10919266792544793792)
XLA Ops:
  0.0 0.7 broadcast_in_dim.7
  0.7 0.6 reshape.9.ids_n
  1.3 102.5 %shard_map.55 = f32[8,8]{1,0:T(8,128)} custom-call(bf16[8,64,4096]{2,1,0:T(8,128)(2,1)} %ri.1, s32[1,64]{1,0:T(1,128)} %bitcast.1, s32[1,128]{1,0:T(1,128)} %reshape.9.ids_n, s32[16]{0:T(128)} %size.1, bf16[1024,1024]{1,0:T(8,128)(2,1)} %go.1, bf16[1024,256]{1,0:T(8,128)(2,1)} %gv.1), custom_call_target="tpu_custom_call" | custom-call | tf_op jit(solution)/shard_map/pallas_call | solution.py:341
  103.9 1.3 %copy.7 = f32[8,8]{1,0:T(8,128)} copy(f32[8,8]{1,0:T(8,128)} %shard_map.55) | data formatting | bytes 512
  (1 shorter events, 0.0 us)

commit v3 on v2

--- a/solution.py
+++ b/solution.py
@@ -13,14 +13,14 @@
 NT = (((1,), (1,)), ((), ()))
 
 
-def gather_kernel(nz, ri, ids_k, ids_n, size, go, gv, out,
-                  slabs, perm, tmp, gop, gvm, sel, dense, virt, flat, idbuf, part, parts,
+def gather_kernel(nz, ri, ids_k, size, go, gv, out,
+                  slabs, perm, tmp, gop, gvm, sel, dense, virt, flat, ids_n, idbuf, part, parts,
                   zsend, zrecv, xsend, xrecv, csend, crecv, isend, irecv, psend, precv, lsem):
     z = lax.axis_index("tensor")
     b = lax.axis_index("batch")
     r = lax.axis_index("rep")
     j = b * 2 + r
-    pieces = 4
+    pieces = 8
     waves = (nz - 1) * pieces
     left = {"tensor": z - 1}
     right = {"tensor": z + 1}
@@ -44,22 +44,20 @@
                                             device_id=dev, device_id_type=MESH)
 
     def spot(o, p, q):
-        return slabs.at[o, q, pl.ds(2 * p, 2)]
+        return slabs.at[o, q, pl.ds(p, 1)]
 
     for q in range(4):
         local(q).start()
     pl.semaphore_wait(barrier, nz - 1 + 3)
 
     def own(p, d):
-        src = ri.at[pl.ds(2 * p, 2), pl.ds(pl.multiple_of(16 * j, 16), 16), :]
+        src = ri.at[pl.ds(p, 1), pl.ds(pl.multiple_of(16 * j, 16), 16), :]
         return remote(src, spot(z, p, j), zsend.at[d, p], zrecv.at[d, p], right if d == 0 else left)
 
     def ids_copy(step):
         dev = {"tensor": lax.rem(z + step, nz)}
         return remote(ids_n, idbuf.at[z], isend.at[step], irecv.at[step], dev)
 
-    for step in range(1, nz):
-        ids_copy(step).start()
     for p in range(pieces):
         @pl.when(z < nz - 1)
         def _():
@@ -68,6 +66,15 @@
         @pl.when(z > 0)
         def _():
             own(p, 1).start()
+
+    slot = lax.broadcasted_iota(jnp.int32, (64, 128), 0)
+    spread_lane = lax.broadcasted_iota(jnp.int32, (64, 128), 1)
+    chosen = jnp.where(slot == (spread_lane // 32) * 16 + spread_lane % 16, 1.0, 0.0).astype(jnp.bfloat16)
+    listed = jnp.broadcast_to(ids_k[...], (8, 64)).astype(jnp.float32).astype(jnp.bfloat16)
+    ids_n[...] = jnp.dot(listed, chosen, preferred_element_type=jnp.float32)[0:1]
+    idbuf[z] = ids_n[...]
+    for step in range(1, nz):
+        ids_copy(step).start()
 
     def origin(d, t):
         return z - 1 - t if d == 0 else z + 1 + t
@@ -149,6 +156,7 @@
         return 0
 
     lax.fori_loop(0, 4, rows_in, 0, unroll=True)
+    arrive(0)
 
     def cols_in(k, _):
         at = pl.ds(pl.multiple_of(k * 256, 256), 256)
@@ -171,7 +179,6 @@
     row = lax.broadcasted_iota(jnp.int32, (256, 64), 0)
     want = (row % 16) * 16 + ((row % 128) // 16) * 2 + row // 128
     sel[...] = jnp.where(ids_k[...] == want, 1.0, 0.0).astype(jnp.bfloat16)
-    idbuf[z] = ids_n[...]
     part[...] = jnp.zeros_like(part)
     for q in range(4):
         local(q).wait()
@@ -225,7 +232,7 @@
 
     def contract(o, p):
         other = jnp.concatenate([slabs[o, q, pl.ds(2 * p, 2)].reshape(32, 4096) for q in range(4)], axis=0)
-        pick = idbuf[o] == want64
+        pick = idbuf[o] == want64.astype(jnp.float32)
         halves = jnp.zeros((8, 128), jnp.float32)
         for m in range(2):
             gram = lax.dot_general(flat[m * 256:(m + 1) * 256, :], other, NT, preferred_element_type=jnp.float32)
@@ -239,58 +246,44 @@
         part[...] += add
 
     def contract_wave(w):
-        t, p = w // pieces, w % pieces
+        t, p = w // 4, w % 4
         for d in (0, 1):
             @pl.when(here(d, t))
             def _():
                 contract(origin(d, t), p)
 
-    def first_phase(w, _):
-        one_function(2 * w)
-        arrive(w)
-
-        @pl.when(w > 0)
-        def _():
-            spread(w - 1)
-        one_function(2 * w + 1)
-        return 0
-
-    lax.fori_loop(0, 4, first_phase, 0)
+    arrive(1)
+
+    def first_phase(f, _):
+        one_function(f)
+        arrive(f + 2)
+        spread(f)
+        return 0
+
+    lax.fori_loop(0, 8, first_phase, 0)
     for step in range(1, nz):
         ids_copy(step).wait_send()
         remote(ids_n, idbuf.at[z], isend.at[step], irecv.at[step], right).wait_recv()
 
     def own_slab(p, _):
         contract(z, p)
-        return 0
-
-    arrive(4)
-    spread(3)
-    lax.fori_loop(0, 2, own_slab, 0)
-    arrive(5)
-    spread(4)
-    lax.fori_loop(2, 4, own_slab, 0)
-
-    def catch_up(w, _):
-        collect(w)
-        contract_wave(w)
-        return 0
-
-    lax.fori_loop(0, 3, catch_up, 0)
-
-    def second_phase(w, _):
-        @pl.when(w < waves)
+        arrive(10 + p)
+        spread(8 + p)
+        return 0
+
+    lax.fori_loop(0, 4, own_slab, 0)
+
+    def second_phase(u, _):
+        @pl.when(u + 14 < waves)
         def _():
-            arrive(w)
-
-        @pl.when(w < waves + 1)
-        def _():
-            spread(w - 1)
-        collect(w - 3)
-        contract_wave(w - 3)
-        return 0
-
-    lax.fori_loop(6, waves + 3, second_phase, 0)
+            arrive(u + 14)
+        spread(u + 12)
+        collect(2 * u)
+        collect(2 * u + 1)
+        contract_wave(u)
+        return 0
+
+    lax.fori_loop(0, waves // 2, second_phase, 0)
 
     def p_copy(k, dev):
         return remote(part, parts.at[k], psend.at[k], precv.at[k], dev)
@@ -333,15 +326,14 @@
 
 
 def fused(nz, ri_tensor, pair_ids, atom_size, green_occ, green_virt):
-    ids_n = jnp.broadcast_to(pair_ids.reshape(4, 1, 16), (4, 2, 16)).reshape(1, 128)
-    waves = (nz - 1) * 4
+    waves = (nz - 1) * 8
     vmem = pl.BlockSpec(memory_space=pltpu.VMEM)
     bf16 = jnp.bfloat16
     dma = pltpu.SemaphoreType.DMA
     return pl.pallas_call(
         functools.partial(gather_kernel, nz),
         out_shape=jax.ShapeDtypeStruct((8, nz * 2), jnp.float32),
-        in_specs=[pl.BlockSpec(memory_space=pl.ANY), vmem, vmem,
+        in_specs=[pl.BlockSpec(memory_space=pl.ANY), vmem,
                   pl.BlockSpec(memory_space=pltpu.SMEM), vmem, vmem],
         out_specs=vmem,
         scratch_shapes=[
@@ -354,17 +346,18 @@
             pltpu.VMEM((1024, 1024), bf16),
             pltpu.VMEM((1024, 256), bf16),
             pltpu.VMEM((512, 4096), bf16),
-            pltpu.VMEM((nz, 1, 128), jnp.int32),
+            pltpu.VMEM((1, 128), jnp.float32),
+            pltpu.VMEM((nz, 1, 128), jnp.float32),
             pltpu.VMEM((8, 128), jnp.float32),
             pltpu.VMEM((3, 8, 128), jnp.float32),
-            dma((2, waves + 4)), dma((2, waves + 4)),
+            dma((2, waves + 8)), dma((2, waves + 8)),
             dma((2, waves)), dma((2, waves)),
             dma((2, waves, 2)), dma((2, waves, 2)),
             dma((nz,)), dma((nz,)), dma((3,)), dma((3,)), dma((4,)),
         ],
         compiler_params=pltpu.CompilerParams(
             collective_id=0, has_side_effects=True, vmem_limit_bytes=56 * 1024 * 1024),
-    )(ri_tensor, pair_ids.reshape(1, 64), ids_n, atom_size, green_occ, green_virt)
+    )(ri_tensor, pair_ids.reshape(1, 64), atom_size, green_occ, green_virt)
 
 
 def per_device(ri_tensor, pair_ids, atom_size, green_occ, green_virt):

time: 105 us -> 97.8 us (0.931)
  the two profiles are of different devices: /device:TPU:0 before, /device:TPU:13 now
where the time goes in v3:
time: 97.8 us; the launch traced here: 97.7 us
  Pallas kernels  96.4 us (99%)
  local copies, waits for them, and re-layouts  1.28 us (1%)
    pallas_call x1, Pallas kernels, fused(): pl.pallas_call(functools.partial(gather_kernel, nz), out_shape=jax.ShapeD...  96.4 us

profile of v3, /device:TPU:13, one launch (start us, length us, event | category | flops | bytes accessed | tf_op | source)
XLA Modules:
  0.0 97.7 jit_solution(3664067559634012874)
XLA Ops:
  0.0 96.4 %shard_map.55 = f32[8,8]{1,0:T(8,128)} custom-call(bf16[8,64,4096]{2,1,0:T(8,128)(2,1)} %ri.1, s32[1,64]{1,0:T(1,128)} %bitcast.1, s32[16]{0:T(128)} %size.1, bf16[1024,1024]{1,0:T(8,128)(2,1)} %go.1, bf16[1024,256]{1,0:T(8,128)(2,1)} %gv.1), custom_call_target="tpu_custom_call" | custom-call | tf_op jit(solution)/shard_map/pallas_call | solution.py:333
  96.4 1.3 %copy.7 = f32[8,8]{1,0:T(8,128)} copy(f32[8,8]{1,0:T(8,128)} %shard_map.55) | data formatting | bytes 512

commit v4 on v3

--- a/solution.py
+++ b/solution.py
@@ -149,6 +149,7 @@
         return 0
 
     lax.fori_loop(0, 8, build, 0)
+    arrive(0)
 
     def rows_in(k, _):
         at = pl.ds(pl.multiple_of(k * 256, 256), 256)
@@ -156,7 +157,7 @@
         return 0
 
     lax.fori_loop(0, 4, rows_in, 0, unroll=True)
-    arrive(0)
+    arrive(1)
 
     def cols_in(k, _):
         at = pl.ds(pl.multiple_of(k * 256, 256), 256)
@@ -252,12 +253,13 @@
             def _():
                 contract(origin(d, t), p)
 
-    arrive(1)
+    arrive(2)
+    spread(0)
 
     def first_phase(f, _):
         one_function(f)
-        arrive(f + 2)
-        spread(f)
+        arrive(f + 3)
+        spread(f + 1)
         return 0
 
     lax.fori_loop(0, 8, first_phase, 0)
@@ -267,17 +269,20 @@
 
     def own_slab(p, _):
         contract(z, p)
-        arrive(10 + p)
-        spread(8 + p)
+        arrive(11 + p)
+        spread(9 + p)
         return 0
 
     lax.fori_loop(0, 4, own_slab, 0)
 
     def second_phase(u, _):
-        @pl.when(u + 14 < waves)
-        def _():
-            arrive(u + 14)
-        spread(u + 12)
+        @pl.when(u + 15 < waves)
+        def _():
+            arrive(u + 15)
+
+        @pl.when(u + 13 < waves)
+        def _():
+            spread(u + 13)
         collect(2 * u)
         collect(2 * u + 1)
         contract_wave(u)

time: 97.8 us -> 100 us (1.022)
  the two profiles are of different devices: /device:TPU:13 before, /device:TPU:11 now
where the time goes in v4:
time: 100 us
  Pallas kernels  99 us (99%)
  local copies, waits for them, and re-layouts  1.28 us (1%)
    pallas_call x1, Pallas kernels, fused(): pl.pallas_call(functools.partial(gather_kernel, nz), out_shape=jax.ShapeD...  99 us

profile of v4, /device:TPU:11, one launch (start us, length us, event | category | flops | bytes accessed | tf_op | source)
XLA Modules:
  0.0 100.3 jit_solution(15668962907371026501)
XLA Ops:
  0.0 99.0 %shard_map.55 = f32[8,8]{1,0:T(8,128)} custom-call(bf16[8,64,4096]{2,1,0:T(8,128)(2,1)} %ri.1, s32[1,64]{1,0:T(1,128)} %bitcast.1, s32[16]{0:T(128)} %size.1, bf16[1024,1024]{1,0:T(8,128)(2,1)} %go.1, bf16[1024,256]{1,0:T(8,128)(2,1)} %gv.1), custom_call_target="tpu_custom_call" | custom-call | tf_op jit(solution)/shard_map/pallas_call | solution.py:338
  99.0 1.3 %copy.7 = f32[8,8]{1,0:T(8,128)} copy(f32[8,8]{1,0:T(8,128)} %shard_map.55) | data formatting | bytes 512

commit v5 on v3

--- a/solution.py
+++ b/solution.py
@@ -110,11 +110,11 @@
             def _():
                 o = origin(d, t)
                 z_in(d, w, o, p).wait_recv()
+                x_copy(d, w, o, p, j).start()
 
                 @pl.when(passes(d, t))
                 def _():
                     z_copy(d, w, o, p).start()
-                x_copy(d, w, o, p, j).start()
                 c_copy(d, w, 0, o, p, j).start()
 
     def spread(w):
@@ -148,7 +148,7 @@
         perm[pl.ds(pl.multiple_of(k * 128, 128), 128), :] = jnp.where(keep, 1.0, 0.0).astype(jnp.bfloat16)
         return 0
 
-    lax.fori_loop(0, 8, build, 0)
+    lax.fori_loop(0, 8, build, 0, unroll=True)
 
     def rows_in(k, _):
         at = pl.ds(pl.multiple_of(k * 256, 256), 256)

time: 97.8 us -> 97.9 us (level)
  the two profiles are of different devices: /device:TPU:13 before, /device:TPU:9 now
where the time goes in v5:
time: 97.9 us; the launch traced here: 97.7 us
  Pallas kernels  96.4 us (98%)
  local copies, waits for them, and re-layouts  1.28 us (1%)
    pallas_call x1, Pallas kernels, fused(): pl.pallas_call(functools.partial(gather_kernel, nz), out_shape=jax.ShapeD...  96.4 us

profile of v5, /device:TPU:9, one launch (start us, length us, event | category | flops | bytes accessed | tf_op | source)
XLA Modules:
  0.0 97.7 jit_solution(3841490351033826384)
XLA Ops:
  0.0 96.4 %shard_map.55 = f32[8,8]{1,0:T(8,128)} custom-call(bf16[8,64,4096]{2,1,0:T(8,128)(2,1)} %ri.1, s32[1,64]{1,0:T(1,128)} %bitcast.1, s32[16]{0:T(128)} %size.1, bf16[1024,1024]{1,0:T(8,128)(2,1)} %go.1, bf16[1024,256]{1,0:T(8,128)(2,1)} %gv.1), custom_call_target="tpu_custom_call" | custom-call | tf_op jit(solution)/shard_map/pallas_call | solution.py:333
  96.5 1.3 %copy.7 = f32[8,8]{1,0:T(8,128)} copy(f32[8,8]{1,0:T(8,128)} %shard_map.55) | data formatting | bytes 512
